TPU v7x, 256 devices: a whole 4x4x8 slice. The times are simulated.
256 devices in a mesh: dp: 4 (over z_hi), expert: 64 (over z_lo, y, x, core).
Axes of the slice: x: 4, y: 4, z: 8 (z_hi: 4, z_lo: 2; z = z_hi * 2 + z_lo), core: 2. Of those that a mesh axis runs over, the one named last changes fastest.
Arguments:
- tokens: bfloat16 [32768, 1024], P(('dp', 'expert')), may hold values from -6 to 6
- cotangent: bfloat16 [32768, 1024], P(('dp', 'expert')), may hold values from -6 to 6
- route: int32 [32768, 2], P(('dp', 'expert')), may hold values from 0 to 63, all different within a row
- gates: float32 [32768, 2], P(('dp', 'expert')), may hold values from 0.2 to 1
- w_up: bfloat16 [64, 1024, 4096], P('expert', None, 'dp'), may hold values from -0.1875 to 0.1875
- w_down: bfloat16 [64, 4096, 1024], P('expert', 'dp'), may hold values from -0.09375 to 0.09375
- moment: bfloat16 [64, 1024, 4096], P('expert', None, 'dp'), may hold values from -24 to 24
- second: bfloat16 [64, 1024, 4096], P('expert', None, 'dp'), may hold values from 4 to 400
Outputs:
- layer_out: bfloat16 [32768, 1024], P(('dp', 'expert'))
- token_grad: bfloat16 [32768, 1024], P(('dp', 'expert'))
- update: bfloat16 [64, 1024, 4096], P('expert', None, 'dp')
Inputs may be any that keep to these rules, and one draw needn't show every extreme that they name: `route`: each row names two different experts; every expert is named by some row.
All inputs are finite; a program needn't handle non-finite values.
Results may differ from a plain program's by a relative error of at most 0.0063.
Values may be sent and summed in bfloat16 or wider, within the bound.
A program may use at most 128 MiB of HBM per device.

v0:
```python
import math

import jax
import jax.numpy as jnp
from jax import lax
from jax.sharding import PartitionSpec as P

beta_first = 0.9
beta_second = 0.999
first_fix = 1.0 - 0.9**10
second_fix = 1.0 - 0.999**10
adam_eps = 1e-08
inv_root_two = 1.0 / math.sqrt(2.0)
inv_root_tau = 1.0 / math.sqrt(2.0 * math.pi)


def gelu_parts(preact):
    normal_cdf = 0.5 * (1.0 + jax.scipy.special.erf(preact * inv_root_two))
    density = jnp.exp(-0.5 * preact * preact) * inv_root_tau
    return (preact * normal_cdf, normal_cdf + preact * density)


def slot_table(route, capacity, experts):
    flat_experts = jnp.concatenate([route[:, 0], route[:, 1]])
    one_hot = (flat_experts[:, None] == jnp.arange(experts, dtype=jnp.int32)[None, :]).astype(
        jnp.int32
    )
    earlier = jnp.cumsum(one_hot, axis=0) - one_hot
    position = jnp.sum(earlier * one_hot, axis=1)
    is_kept = position < capacity
    slot_index = flat_experts * capacity + jnp.minimum(position, capacity - 1)
    return (slot_index, is_kept)


def adam_direction(weight_grad, moment, second):
    first_moment = beta_first * moment.astype(jnp.float32) + (1.0 - beta_first) * weight_grad
    square = (
        beta_second * second.astype(jnp.float32) + (1.0 - beta_second) * weight_grad * weight_grad
    )
    return (first_moment / first_fix / (jnp.sqrt(square / second_fix) + adam_eps)).astype(
        jnp.bfloat16
    )


def contract_last(left, right):
    return lax.dot_general(
        left, right, (((1,), (1,)), ((), ())), preferred_element_type=jnp.float32
    )


def contract_first(left, right):
    return lax.dot_general(
        left, right, (((0,), (0,)), ((), ())), preferred_element_type=jnp.float32
    )


def shards(tokens, cotangent, route, gates, w_up, w_down, moment, second):
    tok_count, model_width = tokens.shape
    experts = lax.axis_size("expert")
    capacity = 2 * tok_count // experts
    local_rows = experts * capacity
    slot_index, is_kept = slot_table(route, capacity, experts)
    cot_float = cotangent.astype(jnp.float32)
    scaled = jnp.concatenate([gates[:, 0:1] * cot_float, gates[:, 1:2] * cot_float], axis=0).astype(
        jnp.bfloat16
    )
    packed_rows = jnp.concatenate([jnp.concatenate([tokens, tokens], axis=0), scaled], axis=1)
    target = jnp.where(is_kept, slot_index, -1)
    selector = (target[None, :] == jnp.arange(local_rows, dtype=jnp.int32)[:, None]).astype(
        jnp.bfloat16
    )
    packed = jnp.dot(selector, packed_rows, preferred_element_type=jnp.float32).astype(jnp.bfloat16)
    packed = packed.reshape(experts, capacity, 2 * model_width)
    arrived = lax.all_to_all(packed, "expert", split_axis=0, concat_axis=0, tiled=True)
    up_proj = w_up[0]
    down_proj = w_down[0]
    gathered = lax.all_gather(arrived, "dp", axis=0, tiled=True).reshape(-1, 2 * model_width)
    inputs = gathered[:, :model_width]
    grad_rows = gathered[:, model_width:]
    preact = jnp.dot(inputs, up_proj, preferred_element_type=jnp.float32)
    hidden_act, gelu_slope = gelu_parts(preact)
    hidden = hidden_act.astype(jnp.bfloat16)
    preact_grad = (contract_last(grad_rows, down_proj) * gelu_slope).astype(jnp.bfloat16)
    weight_grad = contract_first(inputs, preact_grad)
    forward_part = jnp.dot(hidden, down_proj, preferred_element_type=jnp.float32)
    backward_part = contract_last(preact_grad, up_proj)
    summed = lax.psum_scatter(
        jnp.concatenate([forward_part, backward_part], axis=1),
        "dp",
        scatter_dimension=0,
        tiled=True,
    )
    results = summed.astype(jnp.bfloat16)
    returned = lax.all_to_all(
        results.reshape(experts, capacity, 2 * model_width),
        "expert",
        split_axis=0,
        concat_axis=0,
        tiled=True,
    )
    returned = returned.reshape(local_rows, 2 * model_width)
    picked = jnp.where(
        is_kept[:, None], jnp.take(returned, slot_index, axis=0).astype(jnp.float32), 0.0
    )
    first_rows = picked[:tok_count]
    second_rows = picked[tok_count:]
    layer_out = (
        gates[:, 0:1] * first_rows[:, :model_width] + gates[:, 1:2] * second_rows[:, :model_width]
    ).astype(jnp.bfloat16)
    token_grad = (first_rows[:, model_width:] + second_rows[:, model_width:]).astype(jnp.bfloat16)
    update = adam_direction(weight_grad, moment[0], second[0])[None]
    return (layer_out, token_grad, update)


def solution(mesh):
    in_specs = (
        P(("dp", "expert"), None),
        P(("dp", "expert"), None),
        P(("dp", "expert"), None),
        P(("dp", "expert"), None),
        P("expert", None, "dp"),
        P("expert", "dp", None),
        P("expert", None, "dp"),
        P("expert", None, "dp"),
    )
    out_specs = (P(("dp", "expert"), None), P(("dp", "expert"), None), P("expert", None, "dp"))
    return jax.shard_map(shards, mesh=mesh, in_specs=in_specs, out_specs=out_specs, check_vma=False)
```

profile of v0, /device:TPU:32, one launch (start us, length us, event | category | flops | bytes accessed | tf_op | source)
XLA Modules:
  0.0 348.1 jit_solution(16520570543204404426)
XLA Ops:
  7.2 0.0 copy-start
  7.2 0.0 all-gather.2.cloned.1.call-start
  7.2 0.8 slice_bitcast_fusion.1
  8.1 0.8 fusion.47
  8.8 0.6 reduce-window.6
  9.5 0.2 slice_reduce_fusion
  9.7 0.1 fusion.42
  9.8 1.1 fusion.34
  10.9 2.5 convolution_convert_fusion
  13.4 1.5 reshape.126
  14.8 26.3 %all_to_all.10 = bf16[64,4,2048]{2,1,0:T(4,128)(2,1)} all-to-all(bf16[64,4,2048]{2,1,0:T(4,128)(2,1)S(1)} %reshape.126), channel_id=1, replica_groups=mesh['dp'=4,'expert'=64] {'expert'}, dimensions={0} | all-to-all | bytes 2097152 | tf_op jit(solution)/shard_map/all_to_all | solution.py:74
  41.2 0.0 all-gather.2.cloned.1.call-update
  41.2 0.0 reduce-scatter.2.cloned.1.call-start
  41.2 84.8 %all-gather.2.cloned.1.call-done = bf16[256,4,2048]{2,1,0:T(4,128)(2,1)} async-done(((bf16[64,4,2048]{2,1,0:T(4,128)(2,1)}), bf16[256,4,2048]{2,1,0:T(4,128)(2,1)}) %all-gather.2.cloned.1.call-update) | async-done | bytes 4194320 | tf_op jit(solution)/shard_map/all_gather | solution.py:77
  126.1 6.9 %reshape.127 = bf16[1024,2048]{1,0:T(8,128)(2,1)} reshape(bf16[256,4,2048]{2,1,0:T(4,128)(2,1)} %all-gather.2.cloned.1.call-done) | data formatting | bytes 8388608 | tf_op jit(solution)/shard_map/reshape | solution.py:77
  132.9 0.0 copy-start.1
  132.9 4.7 %fusion.19 = f32[1024,1024]{1,0:T(8,128)S(1)} fusion(bf16[1,1024,1024]{2,1,0:T(8,128)(2,1)} %param.12, bf16[1024,2048]{1,0:T(8,128)(2,1)} %reshape.127), kind=kOutput, calls=%fused_computation.27 | convolution fusion | flops 2147483648 | bytes 8388608 | tf_op jit(solution)/shard_map/dot_general | solution.py:80
  137.6 0.0 copy-done
  137.6 0.0 copy-done.1
  137.7 3.8 %fusion.5 = bf16[1024,1024]{1,0:T(8,128)(2,1)S(1)} fusion(f32[1024,1024]{1,0:T(8,128)S(1)} %fusion.19, bf16[1024,2048]{1,0:T(8,128)(2,1)S(1)} %copy-done.1, bf16[1,1024,1024]{2,1,0:T(8,128)(2,1)S(1)} %copy-done), kind=kOutput, calls=%fused_computation.9 | convolution fusion | flops 2157969408 | bytes 10485760 | tf_op jit(solution)/shard_map/dot_general | solution.py:46
  141.5 0.0 copy-start.3
  141.5 0.0 copy-start.2
  141.5 2.7 fusion.13
  144.2 0.0 copy-done.3
  144.3 0.0 copy-done.2
  144.3 2.4 fusion.17
  146.6 4.1 %pad_maximum_fusion = f32[1024,2048]{0,1:T(8,128)} fusion(f32[1024,1024]{0,1:T(8,128)S(1)} %fusion.17, f32[1024,1024]{0,1:T(8,128)S(1)} %fusion.13), kind=kLoop, calls=%fused_computation.1 | loop fusion | flops 2097152 | bytes 16777216 | tf_op jit(solution)/shard_map/concatenate | solution.py:88
  150.7 0.0 reduce-scatter.2.cloned.1.call-update
  150.7 149.7 %reduce-scatter.2.cloned.1.call-done = f32[256,2048]{0,1:T(8,128)} async-done(((f32[1024,2048]{0,1:T(8,128)}), f32[256,2048]{0,1:T(8,128)}) %reduce-scatter.2.cloned.1.call-update) | async-done | bytes 2097168 | tf_op jit(solution)/shard_map/reduce_scatter | solution.py:87
  300.4 1.7 convert_element_type.50
  302.1 1.4 copy.15
  303.6 2.3 reshape.128
  305.8 12.0 %all-to-all-start.1 = ((bf16[64,4,2048]{2,1,0:T(4,128)(2,1)}), bf16[64,4,2048]{2,1,0:T(4,128)(2,1)}, u32[]{:S(2)}, u32[]{:S(2)}) async-start(bf16[64,4,2048]{2,1,0:T(4,128)(2,1)} %reshape.128), calls=%async_computation.2 | async-start | bytes 2097152 | tf_op jit(solution)/shard_map/all_to_all | solution.py:94
  317.9 9.8 %fusion.21 = bf16[1,1024,1024]{2,1,0:T(8,128)(2,1)} fusion(bf16[1,1024,1024]{2,1,0:T(8,128)(2,1)} %param.15, bf16[1,1024,1024]{2,1,0:T(8,128)(2,1)} %param.14, bf16[1024,1024]{1,0:T(8,128)(2,1)} %copy-done.3, bf16[1024,2048]{1,0:T(8,128)(2,1)} %reshape.127), kind=kOutput, calls=%fused_computation.30 | convolution fusion | flops 2162163712 | bytes 10485760 | tf_op jit(solution)/shard_map/dot_general | solution.py:52
  327.7 7.4 %all-to-all-done.1 = bf16[64,4,2048]{2,1,0:T(4,128)(2,1)} async-done(((bf16[64,4,2048]{2,1,0:T(4,128)(2,1)}), bf16[64,4,2048]{2,1,0:T(4,128)(2,1)}, u32[]{:S(2)}, u32[]{:S(2)}) %all-to-all-start.1) | async-done | bytes 1048608 | tf_op jit(solution)/shard_map/all_to_all | solution.py:94
  335.1 1.3 reshape.129
  336.5 2.3 gather_fusion
  338.8 1.5 convert_select_fusion
  340.3 1.0 fusion.36
  (8 shorter events, 0.1 us)
Async XLA Ops:
  7.2 130.5 %copy-start = (bf16[1,1024,1024]{2,1,0:T(8,128)(2,1)S(1)}, bf16[1,1024,1024]{2,1,0:T(8,128)(2,1)}, u32[]{:S(2)}) copy-start(bf16[1,1024,1024]{2,1,0:T(8,128)(2,1)} %param.13) | copy-start | bytes 6291460
  7.2 118.9 %all-gather.2.cloned.1.call-start = ((), (), s32[]{:S(2)}) async-start(), calls=%async_computation.3 | async-start | bytes 5242880 | tf_op jit(solution)/shard_map/all_gather | solution.py:77
  41.2 259.2 %reduce-scatter.2.cloned.1.call-start = ((), (), s32[]{:S(2)}) async-start(), calls=%async_computation.4 | async-start | bytes 10485760 | tf_op jit(solution)/shard_map/reduce_scatter | solution.py:87
  132.9 4.7 %copy-start.1 = (bf16[1024,2048]{1,0:T(8,128)(2,1)S(1)}, bf16[1024,2048]{1,0:T(8,128)(2,1)}, u32[]{:S(2)}) copy-start(bf16[1024,2048]{1,0:T(8,128)(2,1)} %reshape.127) | copy-start | bytes 12582916
  141.5 2.7 copy-start.3
  141.5 2.7 copy-start.2
  305.8 29.3 %all-to-all-start.1 = ((bf16[64,4,2048]{2,1,0:T(4,128)(2,1)}), bf16[64,4,2048]{2,1,0:T(4,128)(2,1)}, u32[]{:S(2)}, u32[]{:S(2)}) async-start(bf16[64,4,2048]{2,1,0:T(4,128)(2,1)} %reshape.128), calls=%async_computation.2 | async-start | bytes 2097152 | tf_op jit(solution)/shard_map/all_to_all | solution.py:94
Sparse Core Ops, SparseCore 0:
  41.3 84.7 all-gather.1
  150.9 149.5 reduce-scatter.1
where the time goes:
time: 350 us; the launch traced here: 348 us
  waiting for transfers between devices  242 us (69%)
  blocking collectives  26.3 us (8%)
  matrix products  25.9 us (7%)
  local copies, waits for them, and re-layouts  17.5 us (5%)
  between operations  14.2 us (4%)
  starting transfers between devices  12.1 us (3%)
  other arithmetic  10.2 us (3%)
    reduce_scatter x1, waiting for transfers between devices, shards(): lax.psum_scatter(jnp.concatenate([forward_part, backward_part], axis=1),...  150 us
    all_gather x1, waiting for transfers between devices, shards(): lax.all_gather(arrived, 'dp', axis=0, tiled=True)  84.8 us
    all_to_all x1, blocking collectives, shards(): lax.all_to_all(packed, 'expert', split_axis=0, concat_axis=0, tiled=True)  26.3 us
    all_to_all x1, starting transfers between devices, shards(): lax.all_to_all(results.reshape(experts, capacity, 2 * model_width), 'expe...  12 us
    dot_general x1, matrix products, contract_first(): lax.dot_general(left, right, (((0,), (0,)), ((), ())), preferred_element_...  9.84 us
    all_to_all x1, waiting for transfers between devices, shards(): lax.all_to_all(results.reshape(experts, capacity, 2 * model_width), 'expe...  7.38 us
  transfers between devices with their start and end apart: 3, of which 3 were waited for; matrix products, arithmetic and copies ran while one was open for 3% of the time, Pallas kernels for 0%

commit v1 on v0

v1 whole, which is shorter than its diff:
```python
import functools
import math

import jax
import jax.numpy as jnp
from jax import lax
from jax.experimental import pallas as pl
from jax.experimental.pallas import tpu as pltpu
from jax.sharding import PartitionSpec as P

beta_first = 0.9
beta_second = 0.999
first_fix = 1.0 - 0.9**10
second_fix = 1.0 - 0.999**10
adam_eps = 1e-08
inv_root_two = 1.0 / math.sqrt(2.0)
inv_root_tau = 1.0 / math.sqrt(2.0 * math.pi)

MESH = pl.DeviceIdType.MESH
F32 = jnp.float32
BF16 = jnp.bfloat16

NZ, NY, NX, NC = 8, 4, 4, 2
PLANE = NY * NX * NC
CAP = 4
TOK = 128
D = 1024
HID = 1024
ROWS = 1024
W = 256
NT = D // W
NQ = 2 * NT
HALF = TOK // 2
BLK = 256

RING = (0, -1, 1, -2, 2, -3, 3, 4)


def ring_at(distance):
    distance = (distance + 3) % NZ - 3
    return RING.index(distance)


def plane_order():
    def load(offset):
        total = [0, 0, 0, 0]
        for axis, step in ((0, offset[1]), (1, offset[0])):
            if step in (1, 2):
                total[2 * axis] += 1
            if step in (3, 2):
                total[2 * axis + 1] += 1
        return total

    rest = [
        (dy, dx, dc)
        for dy in range(NY)
        for dx in range(NX)
        for dc in range(NC)
        if (dy, dx, dc) != (0, 0, 0)
    ]
    now, order = [0, 0, 0, 0], []
    while rest:
        sums = {o: [a + b for a, b in zip(now, load(o))] for o in rest}
        best = min(rest, key=lambda o: (max(sums[o]) - min(sums[o]), -sum(load(o))))
        rest.remove(best)
        now = sums[best]
        order.append(best)
    return order


ORDER = plane_order()
OTHERS = len(ORDER)


def contract_last(left, right):
    return lax.dot_general(left, right, (((1,), (1,)), ((), ())), preferred_element_type=F32)


def contract_first(left, right):
    return lax.dot_general(left, right, (((0,), (0,)), ((), ())), preferred_element_type=F32)


def matmul(left, right):
    return jnp.dot(left, right, preferred_element_type=F32)


def kernel(
    tokens,
    cotangent,
    route,
    gates,
    w_up,
    w_down,
    moment,
    second,
    layer_out,
    token_grad,
    update,
    ring,
    stage,
    inbox,
    outbox,
    back,
    slope,
    hidden,
    up,
    down,
    first_in,
    second_in,
    selector,
    pick,
    slot_gate,
    token_gate,
    meta,
    part,
    sum_send,
    sum_recv,
    load_sem,
    weight_sem,
    store_sem,
    meta_send,
    meta_recv,
    ring_send,
    ring_recv,
    out_send,
    out_recv,
    ret_send,
    ret_recv,
    own_sem,
    sum_ssem,
    sum_rsem,
):
    dp = lax.axis_index("dp")
    expert = lax.axis_index("expert")
    z = dp * 2 + expert // PLANE
    y = (expert // (NX * NC)) % NY
    x = (expert // NC) % NX
    c = expert % NC
    mine = expert % PLANE
    z_lo = z % 2

    def in_ring(distance):
        there = (z + distance + NZ) % NZ
        return (there // 2, (there % 2) * PLANE + mine)

    def in_plane(offset, sign):
        dy, dx, dc = offset
        there = (((y + sign * dy + NY) % NY) * NX + (x + sign * dx + NX) % NX) * NC
        return there + (c + dc) % NC

    def device(place):
        return (dp, z_lo * PLANE + place)

    def rows_of(place):
        return pl.ds(pl.multiple_of(place * 32, 32), 32)

    def load(q):
        source = tokens if q < NT else cotangent
        return pltpu.make_async_copy(
            source.at[:, pl.ds((q % NT) * W, W)], ring.at[q, pl.ds(0, TOK)], load_sem.at[q]
        )

    weight_copies = [
        pltpu.make_async_copy(source.at[0], target, weight_sem.at[i])
        for i, (source, target) in enumerate(
            ((w_up, up), (w_down, down), (moment, first_in), (second, second_in))
        )
    ]
    for q in range(NQ):
        load(q).start()
    weight_copies[0].start()
    weight_copies[1].start()

    barrier = pltpu.get_barrier_semaphore()
    for offset in ORDER:
        pl.semaphore_signal(
            barrier, inc=1, device_id=device(in_plane(offset, 1)), device_id_type=MESH
        )
    for distance in range(1, NZ):
        pl.semaphore_signal(barrier, inc=1, device_id=in_ring(distance), device_id_type=MESH)

    experts = lax.broadcasted_iota(jnp.int32, (2 * PLANE, TOK), 0)
    one_hot = jnp.concatenate(
        [jnp.where(experts == route[k : k + 1, :], 1.0, 0.0) for k in range(2)], axis=1
    )
    before = lax.broadcasted_iota(jnp.int32, (2 * TOK, 2 * TOK), 0) < lax.broadcasted_iota(
        jnp.int32, (2 * TOK, 2 * TOK), 1
    )
    earlier = matmul(one_hot.astype(BF16), jnp.where(before, 1.0, 0.0).astype(BF16))
    position = jnp.sum(earlier * one_hot, axis=0, keepdims=True)
    slots = [
        jnp.where(
            position[:, k * TOK : (k + 1) * TOK] < CAP,
            32.0 * route[k : k + 1, :].astype(F32) + position[:, k * TOK : (k + 1) * TOK],
            -1e6,
        )
        for k in range(2)
    ]
    meta[0] = jnp.concatenate(
        slots + [gates[0:1, :], gates[1:2, :], jnp.zeros((4, TOK), F32)], axis=0
    )
    pl.semaphore_wait(barrier, OTHERS + NZ - 1)

    def ring_copy(q, way, step):
        sign = 1 if way == 0 else -1
        source, target = ring_at(-sign * (step - 1)), ring_at(-sign * step)
        rows, first = (TOK, 0) if step < 4 else (HALF, way * HALF)
        return pltpu.make_async_remote_copy(
            src_ref=ring.at[q, pl.ds(source * TOK + first, rows)],
            dst_ref=ring.at[q, pl.ds(target * TOK + first, rows)],
            send_sem=ring_send.at[q],
            recv_sem=ring_recv.at[(q * 2 + way) * 4 + step - 1],
            device_id=in_ring(sign),
            device_id_type=MESH,
        )

    def gather_step(q, step):
        if step == 1:
            load(q).wait()
        for way in range(2):
            if step > 1:
                ring_copy(q, way, step - 1).wait_recv()
            if step < 5:
                ring_copy(q, way, step).start()

    def meta_copy(distance):
        return pltpu.make_async_remote_copy(
            src_ref=meta.at[0],
            dst_ref=meta.at[ring_at(-distance)],
            send_sem=meta_send,
            recv_sem=meta_recv,
            device_id=in_ring(distance),
            device_id_type=MESH,
        )

    def whole(ref, sem):
        return pltpu.make_async_copy(ref, ref, sem)

    def slot_row(value, at):
        return value + (CAP * at - 1024 * z_lo).astype(F32)

    def build_selector():
        whole(meta.at[pl.ds(1, NZ - 1)], meta_recv).wait()

        @pl.loop(0, ROWS // BLK)
        def _(block):
            first = pl.multiple_of(block * BLK, BLK)
            row = (lax.broadcasted_iota(jnp.int32, (BLK, TOK), 0) + first).astype(F32)
            total = jnp.zeros((BLK, TOK), F32)
            for at in range(NZ):
                hit_0 = row == slot_row(meta[at, 0:1, :], at)
                hit_1 = row == slot_row(meta[at, 1:2, :], at)
                gate = jnp.where(
                    hit_0, meta[at, 2:3, :], jnp.where(hit_1, meta[at, 3:4, :], 0.0)
                )
                selector[pl.ds(first, BLK), pl.ds(at * TOK, TOK)] = jnp.where(
                    hit_0 | hit_1, 1.0, 0.0
                ).astype(BF16)
                total += gate
            slot_gate[pl.ds(first, BLK), :] = jnp.sum(total, axis=1, keepdims=True)

    def build_pick():
        columns = jnp.transpose(
            jnp.concatenate([meta[at] for at in range(NZ)] + [jnp.zeros((64, TOK), F32)], axis=0)
        )
        for at in range(NZ):
            here = pl.ds(at * TOK, TOK)
            column = lax.broadcasted_iota(jnp.int32, (TOK, ROWS), 1).astype(F32)
            for k in range(2):
                slot = slot_row(columns[:, at * 8 + k : at * 8 + k + 1], at)
                pick[k, here, :] = jnp.where(column == slot, 1.0, 0.0).astype(BF16)
                token_gate[k, here, :] = columns[:, at * 8 + 2 + k : at * 8 + 3 + k]

    def out_copy(q, i, offset):
        there = in_plane(offset, 1)
        return pltpu.make_async_remote_copy(
            src_ref=stage.at[q, rows_of(there)],
            dst_ref=inbox.at[q, pl.ds(i * 32, 32)],
            send_sem=out_send.at[q],
            recv_sem=out_recv.at[q],
            device_id=device(there),
            device_id_type=MESH,
        )

    def out_own(q):
        return pltpu.make_async_copy(
            stage.at[q, rows_of(mine)], inbox.at[q, pl.ds(OTHERS * 32, 32)], own_sem.at[q]
        )

    def ret_copy(q, i, offset):
        there = in_plane(offset, -1)
        return pltpu.make_async_remote_copy(
            src_ref=outbox.at[q, pl.ds(i * 32, 32)],
            dst_ref=back.at[q, rows_of(mine)],
            send_sem=ret_send.at[q],
            recv_sem=ret_recv.at[q],
            device_id=device(there),
            device_id_type=MESH,
        )

    def ret_own(q):
        return pltpu.make_async_copy(
            outbox.at[q, pl.ds(OTHERS * 32, 32)], back.at[q, rows_of(mine)], own_sem.at[q]
        )

    def others(ref, q):
        return ref.at[q, pl.ds(0, OTHERS * 32)]

    def dispatch(q):
        @pl.loop(0, ROWS // BLK)
        def _(block):
            here = pl.ds(pl.multiple_of(block * BLK, BLK), BLK)
            rows = matmul(selector[here, :], ring[q])
            if q >= NT:
                rows = rows * slot_gate[here, :]
            stage[q, here, :] = rows.astype(BF16)

        for i, offset in enumerate(ORDER):
            out_copy(q, i, offset).start()
        out_own(q).start()

    def arrived(q):
        whole(others(inbox, q), out_recv.at[q]).wait()
        out_own(q).wait()

    def send_back(q):
        for i, offset in enumerate(ORDER):
            ret_copy(q, i, offset).start()
        ret_own(q).start()

    def returned(q):
        whole(others(back, q), ret_recv.at[q]).wait()
        ret_own(q).wait()

    def forward_rows(block):
        here = pl.ds(block * BLK, BLK)

        @pl.loop(0, HID // BLK)
        def _(column):
            there = pl.ds(pl.multiple_of(column * BLK, BLK), BLK)
            preact = jnp.zeros((BLK, BLK), F32)
            for q in range(NT):
                preact += matmul(inbox[q, here, :], up[pl.ds(q * W, W), there])
            normal_cdf = 0.5 * (1.0 + lax.erf(preact * inv_root_two))
            density = jnp.exp(-0.5 * preact * preact) * inv_root_tau
            hidden[here, there] = (preact * normal_cdf).astype(BF16)
            slope[here, there] = normal_cdf + preact * density

    def forward_part(q):
        @pl.loop(0, ROWS // BLK)
        def _(block):
            here = pl.ds(pl.multiple_of(block * BLK, BLK), BLK)
            outbox[q, here, :] = matmul(hidden[here, :], down[:, pl.ds(q * W, W)]).astype(BF16)

        send_back(q)

    def backward_rows(block):
        here = pl.ds(block * BLK, BLK)

        @pl.loop(0, HID // BLK)
        def _(column):
            there = pl.ds(pl.multiple_of(column * BLK, BLK), BLK)
            grad = jnp.zeros((BLK, BLK), F32)
            for q in range(NT):
                grad += contract_last(inbox[NT + q, here, :], down[there, pl.ds(q * W, W)])
            hidden[here, there] = (grad * slope[here, there]).astype(BF16)

    def backward_part(q):
        @pl.loop(0, ROWS // BLK)
        def _(block):
            here = pl.ds(pl.multiple_of(block * BLK, BLK), BLK)
            outbox[NT + q, here, :] = contract_last(
                hidden[here, :], up[pl.ds(q * W, W), :]
            ).astype(BF16)

        send_back(NT + q)

    def update_rows(q):
        here = pl.ds(q * W, W)

        @pl.loop(0, HID // BLK)
        def _(column):
            there = pl.ds(pl.multiple_of(column * BLK, BLK), BLK)
            grad = contract_first(inbox[q], hidden[:, there])
            first = beta_first * first_in[here, there].astype(F32) + (1.0 - beta_first) * grad
            square = (
                beta_second * second_in[here, there].astype(F32)
                + (1.0 - beta_second) * grad * grad
            )
            first_in[here, there] = (
                first / first_fix / (jnp.sqrt(square / second_fix) + adam_eps)
            ).astype(BF16)

        update_copy(q).start()

    def update_copy(q):
        here = pl.ds(q * W, W)
        return pltpu.make_async_copy(first_in.at[here], update.at[0, here], store_sem.at[q])

    def combine(q):
        @pl.loop(0, ROWS // BLK)
        def _(block):
            here = pl.ds(pl.multiple_of(block * BLK, BLK), BLK)
            if q < NT:
                part[q % 2, here, :] = token_gate[0, here, :] * matmul(
                    pick[0, here, :], back[q]
                ) + token_gate[1, here, :] * matmul(pick[1, here, :], back[q])
            else:
                both = pick[0, here, :] + pick[1, here, :]
                part[q % 2, here, :] = matmul(both, back[q])

    def sum_copy(q, way, step):
        rows, first = (TOK, 0) if step > 1 else (HALF, way * HALF)
        return pltpu.make_async_remote_copy(
            src_ref=sum_send.at[q, way, step - 1, pl.ds(first, rows)],
            dst_ref=sum_recv.at[q, way, step - 1, pl.ds(first, rows)],
            send_sem=sum_ssem.at[q],
            recv_sem=sum_rsem.at[(q * 2 + way) * 4 + step - 1],
            device_id=in_ring(1 if way == 0 else -1),
            device_id_type=MESH,
        )

    def reduce_step(q, step):
        def mine_for(distance, first, rows):
            return part[q % 2, pl.ds(ring_at(distance) * TOK + first, rows), :]

        def got(way, at, first, rows):
            return sum_recv[q, way, at - 1, pl.ds(first, rows), :].astype(F32)

        if step == 5:
            total = mine_for(0, 0, TOK)
            for way in range(2):
                sum_copy(q, way, 4).wait_recv()
                total += got(way, 4, 0, TOK)
            target = layer_out if q < NT else token_grad
            target[:, pl.ds((q % NT) * W, W)] = total.astype(BF16)
            return
        for way in range(2):
            sign = 1 if way == 0 else -1
            first, other = way * HALF, (1 - way) * HALF
            if step == 1:
                sum_send[q, way, 0, pl.ds(first, HALF), :] = mine_for(4, first, HALF).astype(BF16)
            else:
                sum_copy(q, way, step - 1).wait_recv()
                distance = sign * (5 - step)
                if step == 2:
                    sum_send[q, way, 1, pl.ds(first, HALF), :] = (
                        mine_for(distance, first, HALF) + got(way, 1, first, HALF)
                    ).astype(BF16)
                    sum_send[q, way, 1, pl.ds(other, HALF), :] = mine_for(
                        distance, other, HALF
                    ).astype(BF16)
                else:
                    sum_send[q, way, step - 1] = (
                        mine_for(distance, 0, TOK) + got(way, step - 1, 0, TOK)
                    ).astype(BF16)
            sum_copy(q, way, step).start()

    for distance in range(1, NZ):
        meta_copy(distance).start()

    def forward_block(block):
        if block == 0:
            weight_copies[0].wait()
            for q in range(NT):
                arrived(q)
        forward_rows(block)

    filler = {0: [build_selector], 2: [build_pick]}
    for block in range(ROWS // BLK):
        filler[2 * NT + 5 + block] = [functools.partial(forward_block, block)]
    last = 2 * (NQ - 1) + 4
    for tick in range(last + 1):
        for q in range(NQ):
            step = tick - 2 * q + 1
            if 1 <= step <= 5:
                gather_step(q, step)
                if step == 5:
                    dispatch(q)
        for work in filler.pop(tick, ()):
            work()
    for tick in sorted(filler):
        for work in filler[tick]:
            work()

    weight_copies[1].wait()
    weight_copies[2].start()
    weight_copies[3].start()
    for q in range(NT):
        forward_part(q)
    for q in range(NT):
        arrived(NT + q)
    for block in range(ROWS // BLK):
        backward_rows(block)
    for q in range(NT):
        backward_part(q)
    weight_copies[2].wait()
    weight_copies[3].wait()

    for tick in range(last + 1):
        for q in range(NQ):
            step = tick - 2 * q + 1
            if step == 1:
                returned(q)
                combine(q)
            if 1 <= step <= 5:
                reduce_step(q, step)
        if tick % 2 == 1 and tick // 2 < NT:
            update_rows(tick // 2)

    whole(meta.at[pl.ds(1, NZ - 1)], meta_send).wait()
    for q in range(NQ):
        whole(ring.at[q, pl.ds(0, 7 * TOK)], ring_send.at[q]).wait()
        whole(others(stage, q), out_send.at[q]).wait()
        whole(others(outbox, q), ret_send.at[q]).wait()
        whole(ring.at[q, pl.ds(0, 7 * TOK)], sum_ssem.at[q]).wait()
    for q in range(NT):
        update_copy(q).wait()


def shards(tokens, cotangent, route, gates, w_up, w_down, moment, second):
    vmem = pl.BlockSpec(memory_space=pltpu.VMEM)
    anywhere = pl.BlockSpec(memory_space=pl.ANY)
    dma = pltpu.SemaphoreType.DMA
    chunks = pltpu.VMEM((NQ, ROWS, W), BF16)
    return pl.pallas_call(
        kernel,
        out_shape=(
            jax.ShapeDtypeStruct((TOK, D), BF16),
            jax.ShapeDtypeStruct((TOK, D), BF16),
            jax.ShapeDtypeStruct((1, D, HID), BF16),
        ),
        in_specs=[anywhere, anywhere, vmem, vmem, anywhere, anywhere, anywhere, anywhere],
        out_specs=(vmem, vmem, anywhere),
        scratch_shapes=[
            chunks,
            chunks,
            chunks,
            chunks,
            chunks,
            pltpu.VMEM((ROWS, HID), F32),
            pltpu.VMEM((ROWS, HID), BF16),
            pltpu.VMEM((D, HID), BF16),
            pltpu.VMEM((HID, D), BF16),
            pltpu.VMEM((D, HID), BF16),
            pltpu.VMEM((D, HID), BF16),
            pltpu.VMEM((ROWS, ROWS), BF16),
            pltpu.VMEM((2, ROWS, ROWS), BF16),
            pltpu.VMEM((ROWS, 1), F32),
            pltpu.VMEM((2, ROWS, 1), F32),
            pltpu.VMEM((NZ, 8, TOK), F32),
            pltpu.VMEM((2, ROWS, W), F32),
            pltpu.VMEM((NQ, 2, 4, TOK, W), BF16),
            pltpu.VMEM((NQ, 2, 4, TOK, W), BF16),
            dma((NQ,)),
            dma((4,)),
            dma((NT,)),
            dma,
            dma,
            dma((NQ,)),
            dma((NQ * 8,)),
            dma((NQ,)),
            dma((NQ,)),
            dma((NQ,)),
            dma((NQ,)),
            dma((NQ,)),
            dma((NQ,)),
            dma((NQ * 8,)),
        ],
        compiler_params=pltpu.CompilerParams(
            collective_id=0, has_side_effects=True, vmem_limit_bytes=62 << 20
        ),
        cost_estimate=pl.CostEstimate(
            flops=20 * 1024**3, bytes_accessed=12 << 20, transcendentals=3 << 20
        ),
        name="moe_step",
    )(tokens, cotangent, route.T, gates.T, w_up, w_down, moment, second)


def solution(mesh):
    in_specs = (
        P(("dp", "expert"), None),
        P(("dp", "expert"), None),
        P(("dp", "expert"), None),
        P(("dp", "expert"), None),
        P("expert", None, "dp"),
        P("expert", "dp", None),
        P("expert", None, "dp"),
        P("expert", None, "dp"),
    )
    out_specs = (P(("dp", "expert"), None), P(("dp", "expert"), None), P("expert", None, "dp"))
    return jax.shard_map(shards, mesh=mesh, in_specs=in_specs, out_specs=out_specs, check_vma=False)
```

time: 350 us -> 203 us (0.58)
  waiting for transfers between devices: 242 us -> 0 us
  Pallas kernels: 0 us -> 196 us
  blocking collectives: 26.3 us -> 0 us
  matrix products: 25.9 us -> 0 us
  between operations: 14.2 us -> 0.64 us
  starting transfers between devices: 12.1 us -> 0 us
  local copies, waits for them, and re-layouts: 17.5 us -> 6.42 us
  other arithmetic: 10.2 us -> 0 us
    pallas_call x0 -> x1, Pallas kernels: none -> 196 us  [shards(): pl.pallas_call(kernel, out_shape=(jax.ShapeDtypeStruct((TOK, D), BF16), j...]
    reduce_scatter x1 -> x0, waiting for transfers between devices: 150 us -> none  [shards(): lax.psum_scatter(jnp.concatenate([forward_part, backward_part], axis=1),...]
    all_gather x1 -> x0, waiting for transfers between devices: 84.8 us -> none  [shards(): lax.all_gather(arrived, 'dp', axis=0, tiled=True)]
    all_to_all x1 -> x0, blocking collectives: 26.3 us -> none  [shards(): lax.all_to_all(packed, 'expert', split_axis=0, concat_axis=0, tiled=True)]
    dot_general x6 -> x0, matrix products: 25.9 us -> none  [the longest x1 9.84 us: contract_first(): lax.dot_general(left, right, (((0,), (0,)), ((), ())), preferred_element_...]
    all_to_all x1 -> x0, starting transfers between devices: 12 us -> none  [shards(): lax.all_to_all(results.reshape(experts, capacity, 2 * model_width), 'expe...]
    reshape x4 -> x0, local copies, waits for them, and re-layouts: 11.9 us -> none  [the longest x1 6.88 us: shards(): lax.all_gather(arrived, 'dp', axis=0, tiled=True)]
    all_to_all x1 -> x0, waiting for transfers between devices: 7.38 us -> none  [shards(): lax.all_to_all(results.reshape(experts, capacity, 2 * model_width), 'expe...]
  transfers between devices with their start and end apart: 3 -> 0, of which waited for: 3 -> 0; matrix products, arithmetic and copies ran while one was open for 3% -> 0% of each run, Pallas kernels for 0% -> 0%
where the time goes in v1:
time: 203 us
  Pallas kernels  196 us (97%)
  local copies, waits for them, and re-layouts  6.42 us (3%)
    pallas_call x1, Pallas kernels, shards(): pl.pallas_call(kernel, out_shape=(jax.ShapeDtypeStruct((TOK, D), BF16), j...  196 us
    unnamed x3, local copies, waits for them, and re-layouts  6.42 us

profile of v1, /device:TPU:32, one launch (start us, length us, event | category | flops | bytes accessed | tf_op | source)
XLA Modules:
  0.0 202.7 jit_solution(2334586018826795749)
XLA Ops:
  0.6 195.6 %moe_step.1 = (bf16[128,1024]{1,0:T(8,128)(2,1)}, bf16[128,1024]{1,0:T(8,128)(2,1)}, bf16[1,1024,1024]{2,1,0:T(8,128)(2,1)}) custom-call(bf16[128,1024]{1,0:T(8,128)(2,1)} %tokens.1, bf16[128,1024]{1,0:T(8,128)(2,1)} %cotangent.1, s32[2,128]{1,0:T(2,128)} %bitcast.2, f32[2,128]{1,0:T(2,128)} %bitcast.3, bf16[1,1024,1024]{2,1,0:T(8,128)(2,1)} %w_up.1, ...), custom_call_target="tpu_custom_call" | custom-call | flops 21474836480 | bytes 12582912 | tf_op jit(solution)/shard_map/moe_step/pallas_call | solution.py:526
  196.3 1.7 copy.14
  197.9 1.7 copy.15
  199.6 3.1 %copy.16 = bf16[1,1024,1024]{2,1,0:T(8,128)(2,1)} copy(bf16[1,1024,1024]{2,1,0:T(8,128)(2,1)} %get-tuple-element.8) | data formatting | bytes 4194304

commit v2 on v1

--- a/solution.py
+++ b/solution.py
@@ -31,7 +31,9 @@
 NT = D // W
 NQ = 2 * NT
 HALF = TOK // 2
+GROUP = ROWS // 2
 BLK = 256
+PARTS = 4
 
 RING = (0, -1, 1, -2, 2, -3, 3, 4)
 
@@ -151,9 +153,6 @@
     def device(place):
         return (dp, z_lo * PLANE + place)
 
-    def rows_of(place):
-        return pl.ds(pl.multiple_of(place * 32, 32), 32)
-
     def load(q):
         source = tokens if q < NT else cotangent
         return pltpu.make_async_copy(
@@ -191,7 +190,7 @@
     slots = [
         jnp.where(
             position[:, k * TOK : (k + 1) * TOK] < CAP,
-            32.0 * route[k : k + 1, :].astype(F32) + position[:, k * TOK : (k + 1) * TOK],
+            16.0 * route[k : k + 1, :].astype(F32) + position[:, k * TOK : (k + 1) * TOK],
             -1e6,
         )
         for k in range(2)
@@ -237,27 +236,30 @@
         return pltpu.make_async_copy(ref, ref, sem)
 
     def slot_row(value, at):
-        return value + (CAP * at - 1024 * z_lo).astype(F32)
+        return value + (CAP * (at % 4) - GROUP * z_lo).astype(F32)
 
     def build_selector():
         whole(meta.at[pl.ds(1, NZ - 1)], meta_recv).wait()
 
-        @pl.loop(0, ROWS // BLK)
-        def _(block):
-            first = pl.multiple_of(block * BLK, BLK)
-            row = (lax.broadcasted_iota(jnp.int32, (BLK, TOK), 0) + first).astype(F32)
-            total = jnp.zeros((BLK, TOK), F32)
-            for at in range(NZ):
-                hit_0 = row == slot_row(meta[at, 0:1, :], at)
-                hit_1 = row == slot_row(meta[at, 1:2, :], at)
-                gate = jnp.where(
-                    hit_0, meta[at, 2:3, :], jnp.where(hit_1, meta[at, 3:4, :], 0.0)
-                )
-                selector[pl.ds(first, BLK), pl.ds(at * TOK, TOK)] = jnp.where(
-                    hit_0 | hit_1, 1.0, 0.0
-                ).astype(BF16)
-                total += gate
-            slot_gate[pl.ds(first, BLK), :] = jnp.sum(total, axis=1, keepdims=True)
+        for half in range(2):
+
+            @pl.loop(0, GROUP // BLK)
+            def _(block):
+                first = pl.multiple_of(block * BLK, BLK)
+                here = pl.ds(pl.multiple_of(half * GROUP + block * BLK, BLK), BLK)
+                row = (lax.broadcasted_iota(jnp.int32, (BLK, TOK), 0) + first).astype(F32)
+                total = jnp.zeros((BLK, TOK), F32)
+                for i in range(4):
+                    at = half * 4 + i
+                    hit_0 = row == slot_row(meta[at, 0:1, :], at)
+                    hit_1 = row == slot_row(meta[at, 1:2, :], at)
+                    selector[here, pl.ds(i * TOK, TOK)] = jnp.where(
+                        hit_0 | hit_1, 1.0, 0.0
+                    ).astype(BF16)
+                    total += jnp.where(
+                        hit_0, meta[at, 2:3, :], jnp.where(hit_1, meta[at, 3:4, :], 0.0)
+                    )
+                slot_gate[here, :] = jnp.sum(total, axis=1, keepdims=True)
 
     def build_pick():
         columns = jnp.transpose(
@@ -265,72 +267,81 @@
         )
         for at in range(NZ):
             here = pl.ds(at * TOK, TOK)
-            column = lax.broadcasted_iota(jnp.int32, (TOK, ROWS), 1).astype(F32)
+            column = lax.broadcasted_iota(jnp.int32, (TOK, GROUP), 1).astype(F32)
             for k in range(2):
                 slot = slot_row(columns[:, at * 8 + k : at * 8 + k + 1], at)
                 pick[k, here, :] = jnp.where(column == slot, 1.0, 0.0).astype(BF16)
                 token_gate[k, here, :] = columns[:, at * 8 + 2 + k : at * 8 + 3 + k]
 
-    def out_copy(q, i, offset):
+    def slots_of(half, place):
+        return pl.ds(pl.multiple_of(half * GROUP + place * 16, 16), 16)
+
+    def out_copy(q, half, i, offset):
         there = in_plane(offset, 1)
         return pltpu.make_async_remote_copy(
-            src_ref=stage.at[q, rows_of(there)],
-            dst_ref=inbox.at[q, pl.ds(i * 32, 32)],
-            send_sem=out_send.at[q],
-            recv_sem=out_recv.at[q],
+            src_ref=stage.at[q, slots_of(half, there)],
+            dst_ref=inbox.at[q, pl.ds(half * GROUP + i * 16, 16)],
+            send_sem=out_send.at[q * 2 + half],
+            recv_sem=out_recv.at[q * 2 + half],
             device_id=device(there),
             device_id_type=MESH,
         )
 
-    def out_own(q):
+    def out_own(q, half):
         return pltpu.make_async_copy(
-            stage.at[q, rows_of(mine)], inbox.at[q, pl.ds(OTHERS * 32, 32)], own_sem.at[q]
-        )
-
-    def ret_copy(q, i, offset):
+            stage.at[q, slots_of(half, mine)],
+            inbox.at[q, pl.ds(half * GROUP + OTHERS * 16, 16)],
+            own_sem.at[q * 2 + half],
+        )
+
+    def ret_copy(q, half, i, offset):
         there = in_plane(offset, -1)
         return pltpu.make_async_remote_copy(
-            src_ref=outbox.at[q, pl.ds(i * 32, 32)],
-            dst_ref=back.at[q, rows_of(mine)],
-            send_sem=ret_send.at[q],
-            recv_sem=ret_recv.at[q],
+            src_ref=outbox.at[q, pl.ds(half * GROUP + i * 16, 16)],
+            dst_ref=back.at[q, slots_of(half, mine)],
+            send_sem=ret_send.at[q * 2 + half],
+            recv_sem=ret_recv.at[q * 2 + half],
             device_id=device(there),
             device_id_type=MESH,
         )
 
-    def ret_own(q):
+    def ret_own(q, half):
         return pltpu.make_async_copy(
-            outbox.at[q, pl.ds(OTHERS * 32, 32)], back.at[q, rows_of(mine)], own_sem.at[q]
-        )
-
-    def others(ref, q):
-        return ref.at[q, pl.ds(0, OTHERS * 32)]
-
-    def dispatch(q):
-        @pl.loop(0, ROWS // BLK)
+            outbox.at[q, pl.ds(half * GROUP + OTHERS * 16, 16)],
+            back.at[q, slots_of(half, mine)],
+            own_sem.at[q * 2 + half],
+        )
+
+    def others(ref, q, half):
+        return ref.at[q, pl.ds(half * GROUP, OTHERS * 16)]
+
+    def dispatch(q, half):
+        @pl.loop(0, GROUP // BLK)
         def _(block):
-            here = pl.ds(pl.multiple_of(block * BLK, BLK), BLK)
-            rows = matmul(selector[here, :], ring[q])
+            here = pl.ds(pl.multiple_of(half * GROUP + block * BLK, BLK), BLK)
+            rows = matmul(selector[here, :], ring[q, pl.ds(half * GROUP, GROUP), :])
             if q >= NT:
                 rows = rows * slot_gate[here, :]
             stage[q, here, :] = rows.astype(BF16)
 
         for i, offset in enumerate(ORDER):
-            out_copy(q, i, offset).start()
-        out_own(q).start()
+            out_copy(q, half, i, offset).start()
+        out_own(q, half).start()
 
     def arrived(q):
-        whole(others(inbox, q), out_recv.at[q]).wait()
-        out_own(q).wait()
+        for half in range(2):
+            whole(others(inbox, q, half), out_recv.at[q * 2 + half]).wait()
+            out_own(q, half).wait()
 
     def send_back(q):
-        for i, offset in enumerate(ORDER):
-            ret_copy(q, i, offset).start()
-        ret_own(q).start()
-
-    def returned(q):
-        whole(others(back, q), ret_recv.at[q]).wait()
-        ret_own(q).wait()
+        for half in (1, 0):
+            for i, offset in enumerate(ORDER):
+                ret_copy(q, half, i, offset).start()
+            ret_own(q, half).start()
+
+    def returned(q, half):
+        whole(others(back, q, half), ret_recv.at[q * 2 + half]).wait()
+        ret_own(q, half).wait()
 
     def forward_rows(block):
         here = pl.ds(block * BLK, BLK)
@@ -375,10 +386,10 @@
 
         send_back(NT + q)
 
-    def update_rows(q):
+    def update_rows(q, half):
         here = pl.ds(q * W, W)
 
-        @pl.loop(0, HID // BLK)
+        @pl.loop(half * (HID // BLK // 2), (half + 1) * (HID // BLK // 2))
         def _(column):
             there = pl.ds(pl.multiple_of(column * BLK, BLK), BLK)
             grad = contract_first(inbox[q], hidden[:, there])
@@ -391,23 +402,26 @@
                 first / first_fix / (jnp.sqrt(square / second_fix) + adam_eps)
             ).astype(BF16)
 
-        update_copy(q).start()
+        if half == 1:
+            update_copy(q).start()
 
     def update_copy(q):
         here = pl.ds(q * W, W)
         return pltpu.make_async_copy(first_in.at[here], update.at[0, here], store_sem.at[q])
 
-    def combine(q):
-        @pl.loop(0, ROWS // BLK)
+    def combine(q, half):
+        rows = back.at[q, pl.ds(half * GROUP, GROUP)]
+
+        @pl.loop(0, GROUP // BLK)
         def _(block):
-            here = pl.ds(pl.multiple_of(block * BLK, BLK), BLK)
+            here = pl.ds(pl.multiple_of(half * GROUP + block * BLK, BLK), BLK)
             if q < NT:
-                part[q % 2, here, :] = token_gate[0, here, :] * matmul(
-                    pick[0, here, :], back[q]
-                ) + token_gate[1, here, :] * matmul(pick[1, here, :], back[q])
+                part[q % PARTS, here, :] = token_gate[0, here, :] * matmul(
+                    pick[0, here, :], rows[...]
+                ) + token_gate[1, here, :] * matmul(pick[1, here, :], rows[...])
             else:
                 both = pick[0, here, :] + pick[1, here, :]
-                part[q % 2, here, :] = matmul(both, back[q])
+                part[q % PARTS, here, :] = matmul(both, rows[...])
 
     def sum_copy(q, way, step):
         rows, first = (TOK, 0) if step > 1 else (HALF, way * HALF)
@@ -422,7 +436,7 @@
 
     def reduce_step(q, step):
         def mine_for(distance, first, rows):
-            return part[q % 2, pl.ds(ring_at(distance) * TOK + first, rows), :]
+            return part[q % PARTS, pl.ds(ring_at(distance) * TOK + first, rows), :]
 
         def got(way, at, first, rows):
             return sum_recv[q, way, at - 1, pl.ds(first, rows), :].astype(F32)
@@ -466,17 +480,17 @@
                 arrived(q)
         forward_rows(block)
 
-    filler = {0: [build_selector], 2: [build_pick]}
+    filler = {0: [build_selector]}
     for block in range(ROWS // BLK):
-        filler[2 * NT + 5 + block] = [functools.partial(forward_block, block)]
-    last = 2 * (NQ - 1) + 4
+        filler[NT + 5 + block] = [functools.partial(forward_block, block)]
+    last = NQ + 3
     for tick in range(last + 1):
-        for q in range(NQ):
-            step = tick - 2 * q + 1
-            if 1 <= step <= 5:
-                gather_step(q, step)
-                if step == 5:
-                    dispatch(q)
+        steps = [(q, tick - q + 1) for q in range(NQ) if 1 <= tick - q + 1 <= 5]
+        for q, step in steps:
+            gather_step(q, step)
+        for q, step in steps:
+            if step in (3, 5):
+                dispatch(q, 0 if step == 3 else 1)
         for work in filler.pop(tick, ()):
             work()
     for tick in sorted(filler):
@@ -488,6 +502,7 @@
     weight_copies[3].start()
     for q in range(NT):
         forward_part(q)
+    build_pick()
     for q in range(NT):
         arrived(NT + q)
     for block in range(ROWS // BLK):
@@ -499,20 +514,22 @@
 
     for tick in range(last + 1):
         for q in range(NQ):
-            step = tick - 2 * q + 1
-            if step == 1:
-                returned(q)
-                combine(q)
+            step = tick - q + 1
+            if step == 1 or step == 3:
+                half = 1 if step == 1 else 0
+                returned(q, half)
+                combine(q, half)
             if 1 <= step <= 5:
                 reduce_step(q, step)
-        if tick % 2 == 1 and tick // 2 < NT:
-            update_rows(tick // 2)
+        if tick < 2 * NT:
+            update_rows(tick // 2, tick % 2)
 
     whole(meta.at[pl.ds(1, NZ - 1)], meta_send).wait()
     for q in range(NQ):
         whole(ring.at[q, pl.ds(0, 7 * TOK)], ring_send.at[q]).wait()
-        whole(others(stage, q), out_send.at[q]).wait()
-        whole(others(outbox, q), ret_send.at[q]).wait()
+        for half in range(2):
+            whole(others(stage, q, half), out_send.at[q * 2 + half]).wait()
+            whole(others(outbox, q, half), ret_send.at[q * 2 + half]).wait()
         whole(ring.at[q, pl.ds(0, 7 * TOK)], sum_ssem.at[q]).wait()
     for q in range(NT):
         update_copy(q).wait()
@@ -544,12 +561,12 @@
             pltpu.VMEM((HID, D), BF16),
             pltpu.VMEM((D, HID), BF16),
             pltpu.VMEM((D, HID), BF16),
-            pltpu.VMEM((ROWS, ROWS), BF16),
-            pltpu.VMEM((2, ROWS, ROWS), BF16),
+            pltpu.VMEM((ROWS, GROUP), BF16),
+            pltpu.VMEM((2, ROWS, GROUP), BF16),
             pltpu.VMEM((ROWS, 1), F32),
             pltpu.VMEM((2, ROWS, 1), F32),
             pltpu.VMEM((NZ, 8, TOK), F32),
-            pltpu.VMEM((2, ROWS, W), F32),
+            pltpu.VMEM((PARTS, ROWS, W), F32),
             pltpu.VMEM((NQ, 2, 4, TOK, W), BF16),
             pltpu.VMEM((NQ, 2, 4, TOK, W), BF16),
             dma((NQ,)),
@@ -559,11 +576,11 @@
             dma,
             dma((NQ,)),
             dma((NQ * 8,)),
-            dma((NQ,)),
-            dma((NQ,)),
-            dma((NQ,)),
-            dma((NQ,)),
-            dma((NQ,)),
+            dma((NQ * 2,)),
+            dma((NQ * 2,)),
+            dma((NQ * 2,)),
+            dma((NQ * 2,)),
+            dma((NQ * 2,)),
             dma((NQ,)),
             dma((NQ * 8,)),
         ],

time: 203 us -> 149 us (0.73)
  Pallas kernels: 196 us -> 141 us
    pallas_call x1, Pallas kernels: 196 us -> 141 us  [shards(): pl.pallas_call(kernel, out_shape=(jax.ShapeDtypeStruct((TOK, D), BF16), j...]
where the time goes in v2:
time: 149 us; the launch traced here: 148 us
  Pallas kernels  141 us (95%)
  local copies, waits for them, and re-layouts  6.42 us (4%)
    pallas_call x1, Pallas kernels, shards(): pl.pallas_call(kernel, out_shape=(jax.ShapeDtypeStruct((TOK, D), BF16), j...  141 us
    unnamed x3, local copies, waits for them, and re-layouts  6.42 us

profile of v2, /device:TPU:32, one launch (start us, length us, event | category | flops | bytes accessed | tf_op | source)
XLA Modules:
  0.0 148.2 jit_solution(74157801605981208)
XLA Ops:
  0.6 141.2 %moe_step.1 = (bf16[128,1024]{1,0:T(8,128)(2,1)}, bf16[128,1024]{1,0:T(8,128)(2,1)}, bf16[1,1024,1024]{2,1,0:T(8,128)(2,1)}) custom-call(bf16[128,1024]{1,0:T(8,128)(2,1)} %tokens.1, bf16[128,1024]{1,0:T(8,128)(2,1)} %cotangent.1, s32[2,128]{1,0:T(2,128)} %bitcast.2, f32[2,128]{1,0:T(2,128)} %bitcast.3, bf16[1,1024,1024]{2,1,0:T(8,128)(2,1)} %w_up.1, ...), custom_call_target="tpu_custom_call" | custom-call | flops 21474836480 | bytes 12582912 | tf_op jit(solution)/shard_map/moe_step/pallas_call | solution.py:543
  141.8 1.7 %copy.14 = bf16[128,1024]{1,0:T(8,128)(2,1)} copy(bf16[128,1024]{1,0:T(8,128)(2,1)} %get-tuple-element.6) | data formatting | bytes 524288
  143.5 1.7 %copy.15 = bf16[128,1024]{1,0:T(8,128)(2,1)} copy(bf16[128,1024]{1,0:T(8,128)(2,1)} %get-tuple-element.7) | data formatting | bytes 524288
  145.1 3.1 %copy.16 = bf16[1,1024,1024]{2,1,0:T(8,128)(2,1)} copy(bf16[1,1024,1024]{2,1,0:T(8,128)(2,1)} %get-tuple-element.8) | data formatting | bytes 4194304

commit v3 on v2

--- a/solution.py
+++ b/solution.py
@@ -33,7 +33,7 @@
 HALF = TOK // 2
 GROUP = ROWS // 2
 BLK = 256
-PARTS = 4
+PARTS = 8
 
 RING = (0, -1, 1, -2, 2, -3, 3, 4)
 
@@ -95,8 +95,7 @@
     w_down,
     moment,
     second,
-    layer_out,
-    token_grad,
+    result,
     update,
     ring,
     stage,
@@ -446,8 +445,7 @@
             for way in range(2):
                 sum_copy(q, way, 4).wait_recv()
                 total += got(way, 4, 0, TOK)
-            target = layer_out if q < NT else token_grad
-            target[:, pl.ds((q % NT) * W, W)] = total.astype(BF16)
+            result[pl.ds(q // NT * TOK, TOK), pl.ds((q % NT) * W, W)] = total.astype(BF16)
             return
         for way in range(2):
             sign = 1 if way == 0 else -1
@@ -512,9 +510,10 @@
     weight_copies[2].wait()
     weight_copies[3].wait()
 
-    for tick in range(last + 1):
+    begin = [0 if q < NT else q - 2 for q in range(NQ)]
+    for tick in range(max(begin) + 5):
         for q in range(NQ):
-            step = tick - q + 1
+            step = tick - begin[q] + 1
             if step == 1 or step == 3:
                 half = 1 if step == 1 else 0
                 returned(q, half)
@@ -540,15 +539,14 @@
     anywhere = pl.BlockSpec(memory_space=pl.ANY)
     dma = pltpu.SemaphoreType.DMA
     chunks = pltpu.VMEM((NQ, ROWS, W), BF16)
-    return pl.pallas_call(
+    result, update = pl.pallas_call(
         kernel,
         out_shape=(
-            jax.ShapeDtypeStruct((TOK, D), BF16),
-            jax.ShapeDtypeStruct((TOK, D), BF16),
+            jax.ShapeDtypeStruct((2 * TOK, D), BF16),
             jax.ShapeDtypeStruct((1, D, HID), BF16),
         ),
         in_specs=[anywhere, anywhere, vmem, vmem, anywhere, anywhere, anywhere, anywhere],
-        out_specs=(vmem, vmem, anywhere),
+        out_specs=(vmem, anywhere),
         scratch_shapes=[
             chunks,
             chunks,
@@ -592,6 +590,7 @@
         ),
         name="moe_step",
     )(tokens, cotangent, route.T, gates.T, w_up, w_down, moment, second)
+    return (result[:TOK], result[TOK:], update)
 
 
 def solution(mesh):

time: 149 us -> 151 us (1.013)
  Pallas kernels: 141 us -> 145 us
    pallas_call x1, Pallas kernels: 141 us -> 145 us  [shards(): pl.pallas_call(kernel, out_shape=(jax.ShapeDtypeStruct((2 * TOK, D), BF16...]
    unnamed x3 -> x1, local copies, waits for them, and re-layouts: 6.42 us -> 3.08 us
    slice x0 -> x1, local copies, waits for them, and re-layouts: none -> 1.85 us  [shards(): return (result[:TOK], result[TOK:], update)]
where the time goes in v3:
time: 151 us; the launch traced here: 150 us
  Pallas kernels  145 us (96%)
  local copies, waits for them, and re-layouts  4.93 us (3%)
    pallas_call x1, Pallas kernels, shards(): pl.pallas_call(kernel, out_shape=(jax.ShapeDtypeStruct((2 * TOK, D), BF16...  145 us
    unnamed x1, local copies, waits for them, and re-layouts  3.08 us

profile of v3, /device:TPU:32, one launch (start us, length us, event | category | flops | bytes accessed | tf_op | source)
XLA Modules:
  0.0 150.5 jit_solution(9552737822422253455)
XLA Ops:
  0.6 144.9 %moe_step.1 = (bf16[256,1024]{1,0:T(8,128)(2,1)}, bf16[1,1024,1024]{2,1,0:T(8,128)(2,1)}) custom-call(bf16[128,1024]{1,0:T(8,128)(2,1)} %tokens.1, bf16[128,1024]{1,0:T(8,128)(2,1)} %cotangent.1, s32[2,128]{1,0:T(2,128)} %bitcast.2, f32[2,128]{1,0:T(2,128)} %bitcast.3, bf16[1,1024,1024]{2,1,0:T(8,128)(2,1)} %w_up.1, bf16[1,1024,1024]{2,1,0:T(8,128)(2,1)} %w_down.1, ...), custom_call_target="tpu_custom_call" | custom-call | flops 21474836480 | bytes 12582912 | tf_op jit(solution)/shard_map/moe_step/pallas_call | solution.py:542
  145.5 1.9 %fusion = (bf16[128,1024]{1,0:T(8,128)(2,1)}, bf16[128,1024]{1,0:T(8,128)(2,1)}) fusion(bf16[256,1024]{1,0:T(8,128)(2,1)} %get-tuple-element.5), kind=kLoop, calls=%fused_computation | loop fusion | bytes 1048576 | tf_op jit(solution)/shard_map/slice | solution.py:593
  147.4 3.1 %copy.12 = bf16[1,1024,1024]{2,1,0:T(8,128)(2,1)} copy(bf16[1,1024,1024]{2,1,0:T(8,128)(2,1)} %get-tuple-element.14) | data formatting | bytes 4194304
